TPU v7x, 512 devices: a whole 4x4x16 slice. The times are simulated.
512 devices in a mesh: ctx: 128 (over y, z_lo, x), tp: 4 (over z_hi, core).
Axes of the slice: x: 4, y: 4, z: 16 (z_hi: 2, z_lo: 8; z = z_hi * 8 + z_lo), core: 2. Of those that a mesh axis runs over, the one named last changes fastest.
Arguments:
- query_proj: bfloat16 [16384, 4096], P('ctx', 'tp'), may hold values from -6 to 6
- key_proj: bfloat16 [16384, 4096], P('ctx', 'tp'), may hold values from -6 to 6
- value_proj: bfloat16 [16384, 4096], P('ctx', 'tp'), may hold values from -6 to 6
- cotangent: bfloat16 [16384, 4096], P('ctx', 'tp'), may hold values from -6 to 6
- filter_taps: float32 [16384, 4096], P('ctx', 'tp'), may hold values from -1 to 1
- short_weights: float32 [3, 3, 4096], P(None, None, 'tp'), may hold values from -3.5 to 3.5
Outputs:
- gated_out: bfloat16 [16384, 4096], P('ctx', 'tp')
- query_grad: bfloat16 [16384, 4096], P('ctx', 'tp')
- key_grad: bfloat16 [16384, 4096], P('ctx', 'tp')
- value_grad: bfloat16 [16384, 4096], P('ctx', 'tp')
- filter_grad: float32 [16384, 4096], P('ctx', 'tp')
- short_grad: float32 [3, 3, 4096], P(None, None, 'tp')
All inputs are finite; a program needn't handle non-finite values.
Results may differ from a plain program's by a relative error of at most 0.0065.
Values may be sent and summed in bfloat16 or wider, within the bound.
A program may use at most 64 MiB of HBM per device.

v0:
```python
import math

import jax
import jax.numpy as jnp
from jax import lax
from jax.sharding import PartitionSpec as P


def from_behind(array, axis, by):
    peers = lax.axis_size(axis)
    pairs = [(i, i + by) for i in range(peers) if 0 <= i + by < peers]
    return lax.ppermute(array, axis, pairs)


def contract(form, left, right):
    return jnp.einsum(
        form, left, right, precision=lax.Precision.HIGHEST, preferred_element_type=jnp.float32
    )


def dft_tables(rows, cols, period):
    row_ids = lax.broadcasted_iota(jnp.int32, (rows, cols), 0)
    col_ids = lax.broadcasted_iota(jnp.int32, (rows, cols), 1)
    angle = 2.0 * math.pi / period * (row_ids * col_ids % period).astype(jnp.float32)
    return (jnp.cos(angle), jnp.sin(angle))


def make_plan(seq_len):
    small_len = int(math.isqrt(2 * seq_len))
    while seq_len % small_len:
        small_len -= 1
    large_len = 2 * seq_len // small_len
    large_cos, large_sin = dft_tables(large_len // 2, large_len, large_len)
    small_cos, small_sin = dft_tables(small_len, small_len, small_len)
    twist_cos, twist_sin = dft_tables(large_len, small_len, small_len * large_len)
    fwd_large = jnp.stack([large_cos, -large_sin], axis=1)
    fwd_small = jnp.stack([jnp.stack([small_cos, -small_sin]), jnp.stack([small_sin, small_cos])])
    inv_small = jnp.stack([jnp.stack([small_cos, small_sin]), jnp.stack([-small_sin, small_cos])])
    inv_large = jnp.stack([large_cos, -large_sin])
    return (small_len, large_len, fwd_large, fwd_small, inv_small, inv_large, twist_cos, twist_sin)


def forward_spec(signal, dft_plan):
    small_len, large_len, fwd_large, fwd_small, inv_small, inv_large, twist_cos, twist_sin = (
        dft_plan
    )
    cube = signal.reshape(signal.shape[0], large_len // 2, small_len)
    section_one = contract("cba,bpk->cpka", cube, fwd_large)
    real_one = section_one[:, 0]
    imag_one = section_one[:, 1]
    section_two = jnp.stack(
        [real_one * twist_cos + imag_one * twist_sin, imag_one * twist_cos - real_one * twist_sin],
        axis=1,
    )
    return contract("cpka,pqaj->cqkj", section_two, fwd_small)


def inverse_half(spec, dft_plan):
    small_len, large_len, fwd_large, fwd_small, inv_small, inv_large, twist_cos, twist_sin = (
        dft_plan
    )
    section_one = contract("cqkj,qpja->cpka", spec, inv_small)
    real_one = section_one[:, 0]
    imag_one = section_one[:, 1]
    section_two = jnp.stack(
        [real_one * twist_cos - imag_one * twist_sin, imag_one * twist_cos + real_one * twist_sin],
        axis=1,
    )
    signal = contract("cpka,pbk->cba", section_two, inv_large)
    return signal.reshape(signal.shape[0], -1) / float(small_len * large_len)


def complex_mul(left, right):
    left_real, left_imag = (left[:, 0], left[:, 1])
    right_real, right_imag = (right[:, 0], right[:, 1])
    return jnp.stack(
        [
            left_real * right_real - left_imag * right_imag,
            left_real * right_imag + left_imag * right_real,
        ],
        axis=1,
    )


def conj_mul(left, right):
    left_real, left_imag = (left[:, 0], left[:, 1])
    right_real, right_imag = (right[:, 0], right[:, 1])
    return jnp.stack(
        [
            left_real * right_real + left_imag * right_imag,
            left_real * right_imag - left_imag * right_real,
        ],
        axis=1,
    )


def conv_forward(prod_chan, filter_spec, dft_plan):
    prod_spec = forward_spec(prod_chan.astype(jnp.float32), dft_plan)
    conv_chan = inverse_half(complex_mul(prod_spec, filter_spec), dft_plan).astype(jnp.bfloat16)
    return (conv_chan, prod_spec)


def conv_backward(grad_chan, filter_spec, prod_spec, dft_plan, grad_scale):
    grad_spec = forward_spec(grad_chan.astype(jnp.float32), dft_plan)
    dconv_chan = inverse_half(conj_mul(filter_spec, grad_spec), dft_plan).astype(jnp.bfloat16)
    dfilter_chan = inverse_half(conj_mul(prod_spec, grad_spec), dft_plan) * grad_scale
    return (dconv_chan, dfilter_chan)


def receive_filter(filter_taps, dft_plan):
    filter_chan = lax.all_to_all(filter_taps.T, "ctx", split_axis=0, concat_axis=1, tiled=True)
    return forward_spec(filter_chan, dft_plan)


def return_filter(dfilter_chan):
    return (
        lax.all_to_all(
            dfilter_chan.astype(jnp.bfloat16), "ctx", split_axis=1, concat_axis=0, tiled=True
        )
        .astype(dfilter_chan.dtype)
        .T
    )


def causal_taps(extended, weights, length, axis):
    rim_rows = len(weights) - 1
    summed = weights[0] * lax.slice_in_dim(extended, rim_rows, rim_rows + length, axis=axis)
    for offset in range(1, len(weights)):
        summed = summed + weights[offset] * lax.slice_in_dim(
            extended, rim_rows - offset, rim_rows - offset + length, axis=axis
        )
    return summed


def reverse_taps(extended, weights, length, axis):
    summed = weights[0] * lax.slice_in_dim(extended, 0, length, axis=axis)
    for offset in range(1, len(weights)):
        summed = summed + weights[offset] * lax.slice_in_dim(
            extended, offset, offset + length, axis=axis
        )
    return summed


def tap_grads(grad_in, extended, tap_count, length, axis):
    rim_rows = tap_count - 1
    rows = [
        jnp.sum(
            grad_in
            * lax.slice_in_dim(extended, rim_rows - offset, rim_rows - offset + length, axis=axis),
            axis=axis,
        )
        for offset in range(tap_count)
    ]
    return jnp.stack(rows, axis=1)


def shards(query_proj, key_proj, value_proj, cotangent, filter_taps, short_weights):
    tokens = query_proj.shape[0]
    tap_count = short_weights.shape[1]
    rim_rows = tap_count - 1
    seq_len = tokens * lax.axis_size("ctx")
    grad_scale = 1.0 / math.sqrt(seq_len)
    dft_plan = make_plan(seq_len)
    stacked = jnp.stack([query_proj, key_proj, value_proj])
    prev_rim = from_behind(stacked[:, tokens - rim_rows :], "ctx", 1)
    extended = jnp.concatenate([prev_rim, stacked], axis=1).astype(jnp.float32)
    weights = [short_weights[:, offset, None, :] for offset in range(tap_count)]
    short_out = causal_taps(extended, weights, tokens, 1)
    product = (short_out[1] * short_out[2]).astype(jnp.bfloat16)
    cot_wide = cotangent.astype(jnp.float32)
    gate_grad = (cot_wide * short_out[0]).astype(jnp.bfloat16)
    filter_spec = receive_filter(filter_taps, dft_plan)
    prod_chan = lax.all_to_all(product.T, "ctx", split_axis=0, concat_axis=1, tiled=True)
    conv_chan, prod_spec = conv_forward(prod_chan, filter_spec, dft_plan)
    conv_tok = lax.all_to_all(conv_chan, "ctx", split_axis=1, concat_axis=0, tiled=True)
    grad_chan = lax.all_to_all(gate_grad.T, "ctx", split_axis=0, concat_axis=1, tiled=True)
    dconv_chan, dfilter_chan = conv_backward(
        grad_chan, filter_spec, prod_spec, dft_plan, grad_scale
    )
    dconv_tok = lax.all_to_all(dconv_chan, "ctx", split_axis=1, concat_axis=0, tiled=True)
    filter_grad = return_filter(dfilter_chan)
    conv_wide = conv_tok.T.astype(jnp.float32)
    dconv_wide = dconv_tok.T.astype(jnp.float32)
    gated = (short_out[0] * conv_wide).astype(jnp.bfloat16)
    token_grads = jnp.stack(
        [cot_wide * conv_wide, dconv_wide * short_out[2], dconv_wide * short_out[1]]
    )
    next_rim = from_behind(token_grads[:, :rim_rows], "ctx", -1)
    grad_ext = jnp.concatenate([token_grads, next_rim], axis=1)
    inputs_grad = reverse_taps(grad_ext, weights, tokens, 1).astype(jnp.bfloat16)
    weight_part = tap_grads(token_grads, extended, tap_count, tokens, 1)
    short_grad = lax.psum(weight_part, "ctx") * grad_scale
    results = (gated, inputs_grad[0], inputs_grad[1], inputs_grad[2])
    return (results[0], results[1], results[2], results[3], filter_grad, short_grad)


def solution(mesh):
    placed = (
        P("ctx", "tp"),
        P("ctx", "tp"),
        P("ctx", "tp"),
        P("ctx", "tp"),
        P("ctx", "tp"),
        P(None, None, "tp"),
    )
    return jax.shard_map(
        shards,
        mesh=mesh,
        in_specs=placed,
        out_specs=(
            P("ctx", "tp"),
            P("ctx", "tp"),
            P("ctx", "tp"),
            P("ctx", "tp"),
            P("ctx", "tp"),
            P(None, None, "tp"),
        ),
        check_vma=False,
    )
```

profile of v0, /device:TPU:256, one launch (start us, length us, event | category | flops | bytes accessed | tf_op | source)
XLA Modules:
  0.0 1284.4 jit_solution(9625832330967187007)
XLA Ops:
  4.9 3.4 collective-permute-start
  10.9 2.0 maximum_convert_fusion
  12.9 2.4 multiply_add_fusion
  17.2 17.1 %all-to-all-start.3 = ((bf16[128,8,128]{2,1,0:T(8,128)(2,1)}), bf16[128,8,128]{2,1,0:T(8,128)(2,1)S(1)}, u32[]{:S(2)}, u32[]{:S(2)}) async-start(bf16[128,8,128]{2,1,0:T(8,128)(2,1)} %fusion.92), calls=%async_computation.3 | async-start | bytes 524288 | tf_op jit(solution)/shard_map/all_to_all | solution.py:176
  34.3 2.0 copy.69
  36.4 18.0 %all-to-all-done.3 = bf16[128,8,128]{2,1,0:T(8,128)(2,1)S(1)} async-done(((bf16[128,8,128]{2,1,0:T(8,128)(2,1)}), bf16[128,8,128]{2,1,0:T(8,128)(2,1)S(1)}, u32[]{:S(2)}, u32[]{:S(2)}) %all-to-all-start.3) | async-done | bytes 262176 | tf_op jit(solution)/shard_map/all_to_all | solution.py:176
  54.4 8.1 all-to-all-start.1
  66.2 3.3 convolution_bitcast_fusion.1
  69.5 23.2 %all-to-all-done.1 = f32[128,8,128]{2,1,0:T(8,128)} async-done(((f32[128,8,128]{2,1,0:T(8,128)}), f32[128,8,128]{2,1,0:T(8,128)}, u32[]{:S(2)}, u32[]{:S(2)}) %all-to-all-start.1) | async-done | bytes 524320 | tf_op jit(solution)/shard_map/all_to_all | solution.py:111
  92.7 3.1 convolution_bitcast_fusion
  96.8 2.0 fusion.36
  98.8 2.0 fusion.30
  101.7 3.9 fusion.39
  108.0 28.0 %all_to_all.78 = bf16[8,128,128]{2,0,1:T(8,128)(2,1)S(1)} all-to-all(bf16[8,128,128]{2,0,1:T(8,128)(2,1)S(1)} %copy.84), channel_id=1, replica_groups=mesh['ctx'=128,'tp'=4] {'ctx'}, dimensions={1} | all-to-all | bytes 524288 | tf_op jit(solution)/shard_map/all_to_all | solution.py:180
  137.1 27.6 %all_to_all.79 = bf16[128,8,128]{2,1,0:T(8,128)(2,1)S(1)} all-to-all(bf16[128,8,128]{2,1,0:T(8,128)(2,1)S(1)} %get-tuple-element.44), channel_id=1, replica_groups=mesh['ctx'=128,'tp'=4] {'ctx'}, dimensions={0} | all-to-all | bytes 524288 | tf_op jit(solution)/shard_map/all_to_all | solution.py:173
  165.9 2.0 fusion.27
  168.7 3.6 fusion.42
  172.3 3.6 fusion.33
  175.9 2.0 multiply_subtract_fusion
  180.3 8.1 all-to-all-start.2
  188.3 2.9 fusion.81
  192.1 16.2 %all-to-all-done.2 = bf16[8,128,128]{2,0,1:T(8,128)(2,1)} async-done(((bf16[8,128,128]{2,0,1:T(8,128)(2,1)}), bf16[8,128,128]{2,0,1:T(8,128)(2,1)}, u32[]{:S(2)}, u32[]{:S(2)}) %all-to-all-start.2) | async-done | bytes 262176 | tf_op jit(solution)/shard_map/all_to_all | solution.py:175
  208.3 7.9 all-to-all-start.5
  216.3 2.0 fusion.84
  219.6 1.9 copy.85
  222.7 13.5 %all-to-all-done.5 = bf16[8,128,128]{2,0,1:T(8,128)(2,1)} async-done(((bf16[8,128,128]{2,0,1:T(8,128)(2,1)}), bf16[8,128,128]{2,0,1:T(8,128)(2,1)}, u32[]{:S(2)}, u32[]{:S(2)}) %all-to-all-start.5) | async-done | bytes 262176 | tf_op jit(solution)/shard_map/all_to_all | solution.py:117
  236.2 1.8 convert_bitcast_fusion
  238.8 2.0 copy.96
  240.9 1.7 copy.86
  242.6 2.2 pad_maximum_fusion
  244.9 5.2 multiply_reduce_fusion.2
  250.1 1029.7 %psum.7 = f32[3,3,1024]{2,0,1:T(4,128)S(1)} all-reduce(f32[3,3,1024]{2,0,1:T(4,128)S(1)} %pad_maximum_fusion.15), channel_id=1, replica_groups=mesh['ctx'=128,'tp'=4] {'ctx'}, use_global_device_ids=true, to_apply=%region_3.4 | all-reduce | flops 9216 | bytes 73728 | tf_op jit(solution)/shard_map/psum | solution.py:192
  (103 shorter events, 30.9 us)
Async XLA Ops:
  0.6 7.7 copy-start.30
  0.6 7.7 copy-start.22
  1.8 7.9 copy-start.11
  3.1 6.6 copy-start.12
  4.3 5.4 copy-start.13
  4.9 4.8 collective-permute-start
  8.3 4.5 copy-start.23
  8.4 4.5 copy-start.25
  8.6 6.7 copy-start.9
  15.3 1.2 copy-start
  17.2 37.2 %all-to-all-start.3 = ((bf16[128,8,128]{2,1,0:T(8,128)(2,1)}), bf16[128,8,128]{2,1,0:T(8,128)(2,1)S(1)}, u32[]{:S(2)}, u32[]{:S(2)}) async-start(bf16[128,8,128]{2,1,0:T(8,128)(2,1)} %fusion.92), calls=%async_computation.3 | async-start | bytes 524288 | tf_op jit(solution)/shard_map/all_to_all | solution.py:176
  54.4 8.4 copy-start.20
  54.4 38.3 %all-to-all-start.1 = ((f32[128,8,128]{2,1,0:T(8,128)}), f32[128,8,128]{2,1,0:T(8,128)}, u32[]{:S(2)}, u32[]{:S(2)}) async-start(f32[128,8,128]{2,1,0:T(8,128)} %bitcast.253), calls=%async_computation.1 | async-start | bytes 1048576 | tf_op jit(solution)/shard_map/all_to_all | solution.py:111
  92.7 3.1 copy-start.8
  95.8 1.0 copy-start.19
  100.7 1.0 copy-start.17
  105.9 30.1 %copy-start.1 = (f32[3,128,1024]{1,2,0:T(8,128)S(1)}, f32[3,128,1024]{1,2,0:T(8,128)}, u32[]{:S(2)}) copy-start(f32[3,128,1024]{1,2,0:T(8,128)} %copy-done) | copy-start | bytes 4718596
  107.8 56.8 %copy-start.15 = (f32[128,1,256]{0,2,1:T(8,128)S(1)}, f32[128,1,256]{0,2,1:T(8,128)}, u32[]{:S(2)}) copy-start(f32[128,1,256]{0,2,1:T(8,128)} %copy-done.14) | copy-start | bytes 393220
  177.9 10.4 copy-start.28
  180.3 36.0 %copy-start.10 = (bf16[128,1024]{0,1:T(8,128)(2,1)S(1)}, bf16[128,1024]{0,1:T(8,128)(2,1)}, u32[]{:S(2)}) copy-start(bf16[128,1024]{0,1:T(8,128)(2,1)} %copy-done.9) | copy-start | bytes 786436
  180.3 28.0 %all-to-all-start.2 = ((bf16[8,128,128]{2,0,1:T(8,128)(2,1)}), bf16[8,128,128]{2,0,1:T(8,128)(2,1)}, u32[]{:S(2)}, u32[]{:S(2)}) async-start(bf16[8,128,128]{2,0,1:T(8,128)(2,1)} %copy.76), calls=%async_computation.2 | async-start | bytes 524288 | tf_op jit(solution)/shard_map/all_to_all | solution.py:175
  208.3 27.9 %all-to-all-start.5 = ((bf16[8,128,128]{2,0,1:T(8,128)(2,1)}), bf16[8,128,128]{2,0,1:T(8,128)(2,1)}, u32[]{:S(2)}, u32[]{:S(2)}) async-start(bf16[8,128,128]{2,0,1:T(8,128)(2,1)} %copy.91), calls=%async_computation.5 | async-start | bytes 524288 | tf_op jit(solution)/shard_map/all_to_all | solution.py:117
  216.2 2.0 copy-start.2
  216.2 2.0 copy-start.4
  218.3 1.3 copy-start.6
  218.3 19.7 %copy-start.21 = (bf16[128,1024]{0,1:T(8,128)(2,1)S(1)}, bf16[128,1024]{0,1:T(8,128)(2,1)}, u32[]{:S(2)}) copy-start(bf16[128,1024]{0,1:T(8,128)(2,1)} %get-tuple-element.51) | copy-start | bytes 786436
  221.4 19.4 %collective-permute-start.1 = (f32[3,2,1024]{2,1,0:T(2,128)S(1)}, f32[3,2,1024]{2,1,0:T(2,128)S(1)}, u32[]{:S(2)}, u32[]{:S(2)}) collective-permute-start(f32[3,2,1024]{2,1,0:T(2,128)S(1)} %copy.85), channel_id=1, source_target_pairs={{4,0},{8,4},{12,8},{16,12},{20,16},{24,20},{28,24},{32,28},{36,32}... | collective-permute-start | bytes 73736 | tf_op jit(solution)/shard_map/ppermute | solution.py:12
  242.6 2.2 copy-start.3
  242.6 2.2 copy-start.5
  242.6 2.3 copy-start.7
  242.6 2.3 copy-start.24
  242.6 2.3 copy-start.26
  (5 other events, 4.5 us)
where the time goes:
time: 1290 us; the launch traced here: 1280 us
  blocking collectives  1090 us (84%)
  waiting for transfers between devices  72 us (6%)
  starting transfers between devices  45.9 us (4%)
  matrix products  29.9 us (2%)
  other arithmetic  26.8 us (2%)
  local copies, waits for them, and re-layouts  23.2 us (2%)
    psum x1, blocking collectives, shards(): short_grad = lax.psum(weight_part, 'ctx') * grad_scale  1030 us
    dot_general x12, matrix products, contract(): jnp.einsum(form, left, right, precision=lax.Precision.HIGHEST, preferred_...  29.9 us
    all_to_all x1, blocking collectives, shards(): lax.all_to_all(dconv_chan, 'ctx', split_axis=1, concat_axis=0, tiled=True)  28 us
    all_to_all x1, blocking collectives, shards(): lax.all_to_all(product.T, 'ctx', split_axis=0, concat_axis=1, tiled=True)  27.6 us
  transfers between devices with their start and end apart: 6, of which 5 were waited for; matrix products, arithmetic and copies ran while one was open for 2% of the time, Pallas kernels for 0%

commit v1 on v0

v1 whole, which is shorter than its diff:
```python
import functools
import math

import jax
import jax.numpy as jnp
import numpy as np
from jax import lax
from jax.experimental import pallas as pl
from jax.experimental.pallas import tpu as pltpu
from jax.sharding import PartitionSpec as P

MESH = pl.DeviceIdType.MESH
LANES = 128
FACTORS = {128: (4, 8, 4), 16: (2, 4, 2), 8: (2, 2, 2)}
FILTER, PRODUCT, GATE, CONV, DCONV, DFILTER = range(6)
F32, BF16 = jnp.float32, jnp.bfloat16


def halves(table):
    high = table.astype(BF16)
    low = (table - high.astype(np.float64)).astype(BF16)
    return high, low


def tables(factors):
    ys, zs, xs = factors
    blocks = ys * zs * xs
    tokens = LANES
    period = 2 * blocks * tokens
    order = np.arange(blocks).reshape(ys, zs, xs).transpose(0, 2, 1).reshape(-1)
    half = np.arange(blocks) + 0.5
    outer = 2.0 * math.pi / (2 * blocks) * np.outer(half, order)
    fwd_outer = np.concatenate([np.cos(outer), -np.sin(outer)], axis=0)
    inv_outer = np.concatenate([np.cos(outer).T, -np.sin(outer).T], axis=1) * (2.0 / period)
    lane = np.arange(tokens)
    inner = 2.0 * math.pi / tokens * (np.outer(lane, lane) % tokens)
    cos, sin = np.cos(inner), np.sin(inner)
    fwd_inner = np.block([[cos, -sin], [sin, cos]])
    inv_inner = np.block([[cos, sin], [-sin, cos]])
    twist = 2.0 * math.pi / period * np.outer(half, lane)
    twists = np.stack([np.cos(twist), np.sin(twist)]).astype(np.float32)
    fwd_outer = np.concatenate(halves(fwd_outer), axis=1)
    return (
        fwd_outer,
        np.stack(halves(fwd_inner)),
        np.stack(halves(inv_inner)),
        np.stack(halves(inv_outer)),
        twists,
    )


def dot(left, right):
    return jnp.dot(left, right, preferred_element_type=F32)


def split(value):
    high = value.astype(BF16)
    return high, (value - high.astype(F32)).astype(BF16)


def kernel(
    factors, scale,
    q_ref, k_ref, v_ref, cot_ref, taps_ref, weights_ref,
    fwd_outer, fwd_inner, inv_inner, inv_outer, twists,
    gated_ref, qgrad_ref, kgrad_ref, vgrad_ref, fgrad_ref, sgrad_ref,
    halo, ext, shorts, pre, z_out, z_in, p_out, p_in, turn, rows, spec_h, spec_x, spec_g,
    part, part_in, plane, plane_in, total_in,
    halo_send, halo_recv, pre_send, pre_recv, z_send, z_recv, p_send, p_recv,
    part_send, part_recv, plane_send, plane_recv, total_send, total_recv,
):
    ys, zs, xs = factors
    blocks = ys * zs * xs
    groups = ys * xs
    tokens = q_ref.shape[0]
    chans = LANES // groups
    inputs = (q_ref, k_ref, v_ref)
    me = lax.axis_index("ctx")
    my_x = lax.rem(me, xs)
    my_z = lax.rem(me // xs, zs)
    my_y = me // (xs * zs)
    my_g = my_y * xs + my_x
    after = lax.rem(me + 1, blocks)
    before = lax.rem(me + blocks - 1, blocks)

    def at_z(z):
        return (my_y * zs + z) * xs + my_x

    def at_g(g):
        return ((g // xs) * zs + my_z) * xs + lax.rem(g, xs)

    def z_peer(step):
        return lax.rem(my_z + step, zs)

    def g_peer(step):
        return lax.rem(my_g + step, groups)

    def lanes(z):
        return pl.ds(pl.multiple_of(z * LANES, LANES), LANES)

    def send(source, target, send_sem, recv_sem, device):
        return pltpu.make_async_remote_copy(
            src_ref=source, dst_ref=target, send_sem=send_sem, recv_sem=recv_sem,
            device_id={"ctx": device}, device_id_type=MESH,
        )

    def z_copy(unit, z):
        return send(z_out.at[unit, z], z_in.at[unit, my_z], z_send.at[unit, z], z_recv.at[unit, my_z], at_z(z))

    def z_arrival(unit, z):
        return send(z_out.at[unit, z], z_in.at[unit, z], z_send.at[unit, z], z_recv.at[unit, z], at_z(z))

    def p_copy(unit, g):
        return send(p_out.at[unit, g], p_in.at[unit, my_g], p_send.at[unit, g], p_recv.at[unit, my_g], at_g(g))

    def p_arrival(unit, g):
        return send(p_out.at[unit, g], p_in.at[unit, g], p_send.at[unit, g], p_recv.at[unit, g], at_g(g))

    barrier = pltpu.get_barrier_semaphore()

    def greet(device):
        pl.semaphore_signal(barrier, inc=1, device_id={"ctx": device}, device_id_type=MESH)

    @pl.loop(1, zs)
    def _(step):
        greet(at_z(z_peer(step)))

    @pl.loop(1, groups)
    def _(step):
        greet(at_g(g_peer(step)))

    greet(after)
    greet(before)

    @pl.loop(0, zs)
    def _(z):
        z_out[FILTER, z] = taps_ref[:, lanes(z)].astype(BF16)

    z_in[FILTER, my_z] = z_out[FILTER, my_z]
    pl.semaphore_wait(barrier, (zs - 1) + (groups - 1) + 2)

    halo_copies = [
        send(inputs[i].at[pl.ds(tokens - 16, 16)], halo.at[i], halo_send.at[i], halo_recv.at[i], after)
        for i in range(3)
    ]
    for copy in halo_copies:
        copy.start()

    @pl.loop(1, zs)
    def _(step):
        z_copy(FILTER, z_peer(step)).start()

    for copy in halo_copies:
        copy.wait()

    follows = (me > 0).astype(F32)
    precedes = (me < blocks - 1).astype(F32)

    def short_conv(i, z):
        edge = halo[i, :, lanes(z)].astype(F32)[8:] * follows
        ext[i, z, pl.ds(0, 8)] = edge
        ext[i, z, pl.ds(8, tokens)] = inputs[i][:, lanes(z)].astype(F32)
        summed = weights_ref[i, pl.ds(0, 1), lanes(z)] * ext[i, z, pl.ds(8, tokens)]
        for tap in (1, 2):
            summed = summed + weights_ref[i, pl.ds(tap, 1), lanes(z)] * ext[i, z, pl.ds(8 - tap, tokens)]
        shorts[i, z] = summed
        return summed

    def make_product(z):
        return (short_conv(1, z) * short_conv(2, z)).astype(BF16)

    def make_gate(z):
        return (cot_ref[:, lanes(z)].astype(F32) * short_conv(0, z)).astype(BF16)

    def spread(unit, make):
        @pl.loop(1, zs)
        def _(step):
            z = z_peer(step)
            z_out[unit, z] = make(z)
            z_copy(unit, z).start()

        z_in[unit, my_z] = make(my_z)

    spread(PRODUCT, make_product)
    spread(GATE, make_gate)

    def turn_in(unit):
        turn[my_z] = z_in[unit, my_z].astype(F32).T

        @pl.loop(1, zs)
        def _(step):
            z = z_peer(zs - step)
            z_arrival(unit, z).wait_recv()
            turn[z] = z_in[unit, z].astype(F32).T

        def packed(g):
            mine = pl.ds(pl.multiple_of(g * chans, chans), chans)
            return turn[:, mine, :].reshape(zs * chans, tokens).astype(BF16)

        @pl.loop(1, groups)
        def _(step):
            g = g_peer(step)
            p_out[unit, g] = packed(g)
            p_copy(unit, g).start()

        p_in[unit, my_g] = packed(my_g)

    def gather_plane(unit):
        @pl.loop(1, groups)
        def _(step):
            p_arrival(unit, g_peer(groups - step)).wait_recv()

        @pl.loop(0, groups)
        def _(g):
            rows[pl.ds(pl.multiple_of(g * zs * chans, zs * chans), zs * chans), :] = p_in[unit, g].astype(F32)

    def forward(spec):
        for c in range(chans):
            signal = rows[pl.ds(c, blocks, stride=chans), :].astype(BF16)
            outer = dot(fwd_outer[...], jnp.concatenate([signal, signal], axis=0))
            real, imag = outer[:blocks], outer[blocks:]
            cos, sin = twists[0], twists[1]
            high, low = split(jnp.concatenate([real * cos + imag * sin, imag * cos - real * sin], axis=1))
            spec[c] = dot(high, fwd_inner[0]) + dot(low, fwd_inner[0]) + dot(high, fwd_inner[1])

    def inverse(multiply, left, right, factor):
        for c in range(chans):
            high, low = split(multiply(left[c], right[c]))
            inner = dot(high, inv_inner[0]) + dot(low, inv_inner[0]) + dot(high, inv_inner[1])
            real, imag = inner[:, :tokens], inner[:, tokens:]
            cos, sin = twists[0], twists[1]
            high, low = split(jnp.concatenate([real * cos - imag * sin, imag * cos + real * sin], axis=0))
            signal = dot(inv_outer[0], high) + dot(inv_outer[1], high) + dot(inv_outer[0], low)
            if factor != 1.0:
                signal = signal * factor
            rows[pl.ds(c, blocks, stride=chans), :] = signal

    def times(left, right):
        lr, li, rr, ri = left[:, :tokens], left[:, tokens:], right[:, :tokens], right[:, tokens:]
        return jnp.concatenate([lr * rr - li * ri, lr * ri + li * rr], axis=1)

    def conj_times(left, right):
        lr, li, rr, ri = left[:, :tokens], left[:, tokens:], right[:, :tokens], right[:, tokens:]
        return jnp.concatenate([lr * rr + li * ri, lr * ri - li * rr], axis=1)

    def spread_plane(unit):
        def packed(g):
            return rows[pl.ds(pl.multiple_of(g * zs * chans, zs * chans), zs * chans), :].astype(BF16)

        @pl.loop(1, groups)
        def _(step):
            g = g_peer(step)
            p_out[unit, g] = packed(g)
            p_copy(unit, g).start()

        p_in[unit, my_g] = packed(my_g)

    def turn_out(unit):
        gather_plane(unit)

        def turned(z):
            picked = [rows[pl.ds(pl.multiple_of(g * zs * chans + z * chans, chans), chans), :] for g in range(groups)]
            return jnp.concatenate(picked, axis=0).T.astype(BF16)

        @pl.loop(1, zs)
        def _(step):
            z = z_peer(step)
            z_out[unit, z] = turned(z)
            z_copy(unit, z).start()

        z_in[unit, my_z] = turned(my_z)

    turn_in(FILTER)
    gather_plane(FILTER)
    forward(spec_h)
    turn_in(PRODUCT)
    gather_plane(PRODUCT)
    forward(spec_x)
    inverse(times, spec_x, spec_h, 1.0)
    spread_plane(CONV)
    turn_in(GATE)
    turn_out(CONV)
    gather_plane(GATE)
    forward(spec_g)
    inverse(conj_times, spec_h, spec_g, 1.0)
    spread_plane(DCONV)
    inverse(conj_times, spec_x, spec_g, scale)
    spread_plane(DFILTER)
    turn_out(DCONV)
    turn_out(DFILTER)

    def z_wait(unit):
        @pl.loop(1, zs)
        def _(step):
            z_arrival(unit, z_peer(zs - step)).wait_recv()

    def edge_copy(i):
        return send(
            pre.at[i, :, pl.ds(0, 8)], pre.at[i, :, pl.ds(tokens, 8)], pre_send.at[i], pre_recv.at[i], before
        )

    def tap_sums(i, z):
        own = pre[i, z, pl.ds(0, tokens)]
        for tap in range(3):
            summed = jnp.sum(own * ext[i, z, pl.ds(8 - tap, tokens)], axis=0, keepdims=True)
            part[z, pl.ds(3 * i + tap, 1)] = summed * scale

    def reverse_conv(i, out_ref):
        @pl.loop(0, zs)
        def _(z):
            pre[i, z, pl.ds(tokens, 8)] = pre[i, z, pl.ds(tokens, 8)] * precedes
            summed = weights_ref[i, pl.ds(0, 1), lanes(z)] * pre[i, z, pl.ds(0, tokens)]
            for tap in (1, 2):
                summed = summed + weights_ref[i, pl.ds(tap, 1), lanes(z)] * pre[i, z, pl.ds(tap, tokens)]
            out_ref[:, lanes(z)] = summed.astype(BF16)

    z_wait(CONV)

    @pl.loop(0, zs)
    def _(z):
        conv = z_in[CONV, z].astype(F32)
        gated_ref[:, lanes(z)] = (shorts[0, z] * conv).astype(BF16)
        pre[0, z, pl.ds(0, tokens)] = cot_ref[:, lanes(z)].astype(F32) * conv

    edge_copy(0).start()

    @pl.loop(0, zs)
    def _(z):
        part[z] = jnp.zeros_like(part[z])
        tap_sums(0, z)

    edge_copy(0).wait()
    reverse_conv(0, qgrad_ref)

    z_wait(DCONV)

    @pl.loop(0, zs)
    def _(z):
        grad = z_in[DCONV, z].astype(F32)
        pre[1, z, pl.ds(0, tokens)] = grad * shorts[2, z]
        pre[2, z, pl.ds(0, tokens)] = grad * shorts[1, z]

    edge_copy(1).start()
    edge_copy(2).start()

    def part_copy(z, slot):
        return send(part.at[z], part_in.at[slot], part_send.at[z], part_recv.at[slot], at_z(z))

    def plane_copy(g, slot):
        return send(plane, plane_in.at[slot], plane_send.at[g], plane_recv.at[slot], at_g(g))

    def total_copy(z, slot):
        return send(plane, total_in.at[slot], total_send.at[z], total_recv.at[slot], at_z(z))

    @pl.loop(0, zs)
    def _(z):
        tap_sums(1, z)
        tap_sums(2, z)

    @pl.loop(1, zs)
    def _(step):
        part_copy(z_peer(step), my_z).start()

    part_in[my_z] = part[my_z]
    edge_copy(1).wait()
    edge_copy(2).wait()
    reverse_conv(1, kgrad_ref)

    @pl.loop(1, zs)
    def _(step):
        z = z_peer(zs - step)
        part_copy(z, z).wait_recv()

    plane[...] = jnp.sum(part_in[...], axis=0)

    @pl.loop(1, groups)
    def _(step):
        plane_copy(g_peer(step), my_g).start()

    plane_in[my_g] = plane[...]
    reverse_conv(2, vgrad_ref)

    @pl.loop(1, groups)
    def _(step):
        g = g_peer(groups - step)
        plane_copy(g, g).wait()

    plane[...] = jnp.sum(plane_in[...], axis=0)

    @pl.loop(1, zs)
    def _(step):
        total_copy(z_peer(step), my_z).start()

    total_in[my_z] = plane[...]

    z_wait(DFILTER)

    @pl.loop(0, zs)
    def _(z):
        fgrad_ref[:, lanes(z)] = z_in[DFILTER, z].astype(F32)

    @pl.loop(1, zs)
    def _(step):
        z = z_peer(zs - step)
        total_copy(z, z).wait()
        part_copy(z, z).wait_send()

    for z in range(zs):
        for i in range(3):
            sgrad_ref[i, :, z * LANES:(z + 1) * LANES] = total_in[z, 3 * i:3 * i + 3]

    @pl.loop(0, 6)
    def _(unit):
        @pl.loop(1, zs)
        def _(step):
            z_copy(unit, z_peer(step)).wait_send()

        @pl.loop(1, groups)
        def _(step):
            p_copy(unit, g_peer(step)).wait_send()


def shards(factors, query_proj, key_proj, value_proj, cotangent, filter_taps, short_weights):
    ys, zs, xs = factors
    blocks = ys * zs * xs
    groups = ys * xs
    tokens, width = query_proj.shape
    chans = LANES // groups
    scale = 1.0 / math.sqrt(blocks * tokens)
    whole = pl.BlockSpec(memory_space=pltpu.VMEM)
    constants = [jnp.asarray(table) for table in tables(factors)]
    scratch = [
        pltpu.VMEM((3, 16, width), BF16),
        pltpu.VMEM((3, zs, tokens + 8, LANES), F32),
        pltpu.VMEM((3, zs, tokens, LANES), F32),
        pltpu.VMEM((3, zs, tokens + 8, LANES), F32),
        pltpu.VMEM((6, zs, tokens, LANES), BF16),
        pltpu.VMEM((6, zs, tokens, LANES), BF16),
        pltpu.VMEM((6, groups, zs * chans, tokens), BF16),
        pltpu.VMEM((6, groups, zs * chans, tokens), BF16),
        pltpu.VMEM((zs, LANES, tokens), F32),
        pltpu.VMEM((blocks * chans, tokens), F32),
        pltpu.VMEM((chans, blocks, 2 * tokens), F32),
        pltpu.VMEM((chans, blocks, 2 * tokens), F32),
        pltpu.VMEM((chans, blocks, 2 * tokens), F32),
        pltpu.VMEM((zs, 16, LANES), F32),
        pltpu.VMEM((zs, 16, LANES), F32),
        pltpu.VMEM((16, LANES), F32),
        pltpu.VMEM((groups, 16, LANES), F32),
        pltpu.VMEM((zs, 16, LANES), F32),
    ]
    for shape in (
        (3,), (3,), (3,), (3,), (6, zs), (6, zs), (6, groups), (6, groups),
        (zs,), (zs,), (groups,), (groups,), (zs,), (zs,),
    ):
        scratch.append(pltpu.SemaphoreType.DMA(shape))
    token_out = jax.ShapeDtypeStruct((tokens, width), BF16)
    return pl.pallas_call(
        functools.partial(kernel, factors, scale),
        out_shape=(
            token_out, token_out, token_out, token_out,
            jax.ShapeDtypeStruct((tokens, width), F32),
            jax.ShapeDtypeStruct(short_weights.shape, F32),
        ),
        in_specs=[whole] * 11,
        out_specs=(whole,) * 6,
        scratch_shapes=scratch,
        compiler_params=pltpu.CompilerParams(
            collective_id=0, has_side_effects=True, vmem_limit_bytes=48 * 1024 * 1024
        ),
    )(query_proj, key_proj, value_proj, cotangent, filter_taps, short_weights, *constants)


def solution(mesh):
    rows = P("ctx", "tp")
    weights = P(None, None, "tp")
    return jax.shard_map(
        functools.partial(shards, FACTORS[mesh.shape["ctx"]]),
        mesh=mesh,
        in_specs=(rows, rows, rows, rows, rows, weights),
        out_specs=(rows, rows, rows, rows, rows, weights),
        check_vma=False,
    )
```

time: 1290 us -> 132 us (0.10)
  the two profiles are of different devices: /device:TPU:256 before, /device:TPU:2 now
where the time goes in v1:
time: 132 us
  Pallas kernels  117 us (89%)
  local copies, waits for them, and re-layouts  14.5 us (11%)
    pallas_call x1, Pallas kernels, shards(): pl.pallas_call(functools.partial(kernel, factors, scale), out_shape=(toke...  117 us
    unnamed x28, local copies, waits for them, and re-layouts  14.5 us

profile of v1, /device:TPU:2, one launch (start us, length us, event | category | flops | bytes accessed | tf_op | source)
XLA Modules:
  0.0 131.6 jit_solution(9167579681251634016)
XLA Ops:
  0.6 0.0 copy-start
  0.6 1.0 copy-done
  1.7 0.0 copy-start.1
  1.7 0.9 copy-done.1
  2.6 0.0 copy-start.2
  2.6 0.9 copy-done.2
  3.6 0.0 copy-start.3
  3.6 0.9 copy-done.3
  4.5 0.0 copy-start.4
  4.5 0.9 copy-done.4
  5.5 0.0 copy-start.5
  5.5 0.9 copy-done.5
  6.4 0.0 copy-start.6
  6.4 0.9 copy-done.6
  7.4 0.0 copy-start.7
  7.4 0.9 copy-done.7
  8.3 0.0 copy-start.8
  8.3 0.9 copy-done.8
  9.2 0.0 copy-start.9
  9.2 0.9 copy-done.9
  10.1 0.0 copy-start.10
  10.1 0.8 copy-done.10
  10.9 116.5 %shard_map.154 = (bf16[128,1024]{1,0:T(8,128)(2,1)S(1)}, bf16[128,1024]{1,0:T(8,128)(2,1)S(1)}, bf16[128,1024]{1,0:T(8,128)(2,1)S(1)}, bf16[128,1024]{1,0:T(8,12...) custom-call(bf16[128,1024]{1,0:T(8,128)(2,1)S(1)} %copy-done.1, bf16[128,1024]{1,0:T(8,128)(2,1)S(1)} %copy-done.2, ...), custom_call_target="tpu_custom_call" | custom-call | tf_op jit(solution)/shard_map/pallas_call | solution.py:457
  127.4 0.7 copy.23
  128.1 0.7 copy.24
  128.8 0.7 copy.25
  129.5 0.7 copy.26
  130.2 0.8 copy.27
  131.0 0.6 copy.28
Async XLA Ops:
  0.6 1.0 copy-start
  1.7 0.9 copy-start.1
  2.6 0.9 copy-start.2
  3.6 0.9 copy-start.3
  4.5 0.9 copy-start.4
  5.5 0.9 copy-start.5
  6.4 0.9 copy-start.6
  7.4 0.9 copy-start.7
  8.3 0.9 copy-start.8
  9.2 0.9 copy-start.9
  10.1 0.8 copy-start.10

commit v2 on v1

--- a/solution.py
+++ b/solution.py
@@ -11,6 +11,7 @@
 
 MESH = pl.DeviceIdType.MESH
 LANES = 128
+VMEM_BYTES = 60 * 1024 * 1024
 FACTORS = {128: (4, 8, 4), 16: (2, 4, 2), 8: (2, 2, 2)}
 FILTER, PRODUCT, GATE, CONV, DCONV, DFILTER = range(6)
 F32, BF16 = jnp.float32, jnp.bfloat16
@@ -60,13 +61,16 @@
 
 def kernel(
     factors, scale,
+    q_hbm, k_hbm, v_hbm, cot_hbm, taps_hbm, weights_hbm,
+    fwd_outer_hbm, fwd_inner_hbm, inv_inner_hbm, inv_outer_hbm, twists_hbm,
+    gated_hbm, qgrad_hbm, kgrad_hbm, vgrad_hbm, fgrad_hbm, sgrad_hbm,
     q_ref, k_ref, v_ref, cot_ref, taps_ref, weights_ref,
     fwd_outer, fwd_inner, inv_inner, inv_outer, twists,
     gated_ref, qgrad_ref, kgrad_ref, vgrad_ref, fgrad_ref, sgrad_ref,
     halo, ext, shorts, pre, z_out, z_in, p_out, p_in, turn, rows, spec_h, spec_x, spec_g,
-    part, part_in, plane, plane_in, total_in,
-    halo_send, halo_recv, pre_send, pre_recv, z_send, z_recv, p_send, p_recv,
-    part_send, part_recv, plane_send, plane_recv, total_send, total_recv,
+    part, part_in, plane, line_in, total, total_in,
+    load, unload, halo_send, halo_recv, pre_send, pre_recv, z_send, z_recv, p_send, p_recv,
+    part_send, part_recv, line_send, line_recv, total_send, total_recv,
 ):
     ys, zs, xs = factors
     blocks = ys * zs * xs
@@ -115,6 +119,25 @@
     def p_arrival(unit, g):
         return send(p_out.at[unit, g], p_in.at[unit, g], p_send.at[unit, g], p_recv.at[unit, g], at_g(g))
 
+    loads = [
+        pltpu.make_async_copy(source, target, load.at[i])
+        for i, (source, target) in enumerate((
+            (taps_hbm, taps_ref), (q_hbm, q_ref), (k_hbm, k_ref), (v_hbm, v_ref), (weights_hbm, weights_ref),
+            (cot_hbm, cot_ref), (fwd_outer_hbm, fwd_outer), (fwd_inner_hbm, fwd_inner), (twists_hbm, twists),
+            (inv_inner_hbm, inv_inner), (inv_outer_hbm, inv_outer),
+        ))
+    ]
+    for copy in loads:
+        copy.start()
+
+    unloads = [
+        pltpu.make_async_copy(source, target, unload.at[i])
+        for i, (source, target) in enumerate((
+            (gated_ref, gated_hbm), (qgrad_ref, qgrad_hbm), (kgrad_ref, kgrad_hbm), (vgrad_ref, vgrad_hbm),
+            (fgrad_ref, fgrad_hbm), (sgrad_ref, sgrad_hbm),
+        ))
+    ]
+
     barrier = pltpu.get_barrier_semaphore()
 
     def greet(device):
@@ -130,12 +153,15 @@
 
     greet(after)
     greet(before)
+    loads[0].wait()
 
     @pl.loop(0, zs)
     def _(z):
         z_out[FILTER, z] = taps_ref[:, lanes(z)].astype(BF16)
 
     z_in[FILTER, my_z] = z_out[FILTER, my_z]
+    for copy in loads[1:6]:
+        copy.wait()
     pl.semaphore_wait(barrier, (zs - 1) + (groups - 1) + 2)
 
     halo_copies = [
@@ -171,31 +197,15 @@
     def make_gate(z):
         return (cot_ref[:, lanes(z)].astype(F32) * short_conv(0, z)).astype(BF16)
 
-    def spread(unit, make):
-        @pl.loop(1, zs)
-        def _(step):
-            z = z_peer(step)
-            z_out[unit, z] = make(z)
-            z_copy(unit, z).start()
-
-        z_in[unit, my_z] = make(my_z)
-
-    spread(PRODUCT, make_product)
-    spread(GATE, make_gate)
-
-    def turn_in(unit):
-        turn[my_z] = z_in[unit, my_z].astype(F32).T
-
-        @pl.loop(1, zs)
-        def _(step):
-            z = z_peer(zs - step)
-            z_arrival(unit, z).wait_recv()
-            turn[z] = z_in[unit, z].astype(F32).T
-
-        def packed(g):
-            mine = pl.ds(pl.multiple_of(g * chans, chans), chans)
-            return turn[:, mine, :].reshape(zs * chans, tokens).astype(BF16)
-
+    def packed(g):
+        mine = pl.ds(pl.multiple_of(g * chans, chans), chans)
+        return turn[:, mine, :].reshape(zs * chans, tokens).astype(BF16)
+
+    def picked(z):
+        parts = [rows[pl.ds(pl.multiple_of((g * zs + z) * chans, chans), chans), :] for g in range(groups)]
+        return jnp.concatenate(parts, axis=0)
+
+    def to_plane(unit):
         @pl.loop(1, groups)
         def _(step):
             g = g_peer(step)
@@ -204,7 +214,7 @@
 
         p_in[unit, my_g] = packed(my_g)
 
-    def gather_plane(unit):
+    def from_plane(unit):
         @pl.loop(1, groups)
         def _(step):
             p_arrival(unit, g_peer(groups - step)).wait_recv()
@@ -212,6 +222,48 @@
         @pl.loop(0, groups)
         def _(g):
             rows[pl.ds(pl.multiple_of(g * zs * chans, zs * chans), zs * chans), :] = p_in[unit, g].astype(F32)
+
+    def to_line(unit, block, held_back=0):
+        @pl.loop(1, zs - held_back)
+        def _(step):
+            z = z_peer(step)
+            z_out[unit, z] = block(z).astype(BF16)
+            z_copy(unit, z).start()
+
+        if held_back:
+            @pl.loop(zs - held_back, zs)
+            def _(step):
+                z = z_peer(step)
+                z_out[unit, z] = block(z).astype(BF16)
+
+        z_in[unit, my_z] = block(my_z).astype(BF16)
+
+    def send_held_back(unit, held_back):
+        @pl.loop(zs - held_back, zs)
+        def _(step):
+            z_copy(unit, z_peer(step)).start()
+
+    def from_line(unit, use):
+        use(my_z, z_in[unit, my_z].astype(F32))
+
+        @pl.loop(1, zs)
+        def _(step):
+            z = z_peer(zs - step)
+            z_arrival(unit, z).wait_recv()
+            use(z, z_in[unit, z].astype(F32))
+
+    def keep(z, block):
+        turn[z] = block
+
+    def keep_turned(z, block):
+        turn[z] = block.T
+
+    def keep_rows(z, block):
+        for g in range(groups):
+            rows[pl.ds(pl.multiple_of((g * zs + z) * chans, chans), chans), :] = block[g * chans:(g + 1) * chans]
+
+    def picked_turned(z):
+        return picked(z).T
 
     def forward(spec):
         for c in range(chans):
@@ -242,51 +294,52 @@
         lr, li, rr, ri = left[:, :tokens], left[:, tokens:], right[:, :tokens], right[:, tokens:]
         return jnp.concatenate([lr * rr + li * ri, lr * ri - li * rr], axis=1)
 
-    def spread_plane(unit):
-        def packed(g):
+    def rows_to_plane(unit):
+        def block(g):
             return rows[pl.ds(pl.multiple_of(g * zs * chans, zs * chans), zs * chans), :].astype(BF16)
 
         @pl.loop(1, groups)
         def _(step):
             g = g_peer(step)
-            p_out[unit, g] = packed(g)
+            p_out[unit, g] = block(g)
             p_copy(unit, g).start()
 
-        p_in[unit, my_g] = packed(my_g)
-
-    def turn_out(unit):
-        gather_plane(unit)
-
-        def turned(z):
-            picked = [rows[pl.ds(pl.multiple_of(g * zs * chans + z * chans, chans), chans), :] for g in range(groups)]
-            return jnp.concatenate(picked, axis=0).T.astype(BF16)
-
-        @pl.loop(1, zs)
-        def _(step):
-            z = z_peer(step)
-            z_out[unit, z] = turned(z)
-            z_copy(unit, z).start()
-
-        z_in[unit, my_z] = turned(my_z)
-
-    turn_in(FILTER)
-    gather_plane(FILTER)
+        p_in[unit, my_g] = block(my_g)
+
+    for unit, make in ((PRODUCT, make_product), (GATE, make_gate)):
+        @pl.loop(0, zs)
+        def _(z):
+            keep_turned(z, make(z).astype(F32))
+
+        to_plane(unit)
+
+    for copy in loads[6:]:
+        copy.wait()
+    from_plane(PRODUCT)
+    to_line(PRODUCT, picked)
+    from_line(FILTER, keep_turned)
+    to_plane(FILTER)
+    from_plane(GATE)
+    to_line(GATE, picked)
+    from_plane(FILTER)
     forward(spec_h)
-    turn_in(PRODUCT)
-    gather_plane(PRODUCT)
+    from_line(PRODUCT, keep_rows)
     forward(spec_x)
     inverse(times, spec_x, spec_h, 1.0)
-    spread_plane(CONV)
-    turn_in(GATE)
-    turn_out(CONV)
-    gather_plane(GATE)
+    to_line(CONV, picked)
+    from_line(GATE, keep_rows)
     forward(spec_g)
     inverse(conj_times, spec_h, spec_g, 1.0)
-    spread_plane(DCONV)
+    rows_to_plane(DCONV)
     inverse(conj_times, spec_x, spec_g, scale)
-    spread_plane(DFILTER)
-    turn_out(DCONV)
-    turn_out(DFILTER)
+    rows_to_plane(DFILTER)
+    from_plane(DCONV)
+    to_line(DCONV, picked_turned)
+    from_plane(DFILTER)
+    late = 3 * zs // 8
+    to_line(DFILTER, picked_turned, late)
+    from_line(CONV, keep)
+    to_plane(CONV)
 
     def z_wait(unit):
         @pl.loop(1, zs)
@@ -302,7 +355,7 @@
         own = pre[i, z, pl.ds(0, tokens)]
         for tap in range(3):
             summed = jnp.sum(own * ext[i, z, pl.ds(8 - tap, tokens)], axis=0, keepdims=True)
-            part[z, pl.ds(3 * i + tap, 1)] = summed * scale
+            part[3 * i + tap, pl.ds(z, 1)] = summed * scale
 
     def reverse_conv(i, out_ref):
         @pl.loop(0, zs)
@@ -313,23 +366,25 @@
                 summed = summed + weights_ref[i, pl.ds(tap, 1), lanes(z)] * pre[i, z, pl.ds(tap, tokens)]
             out_ref[:, lanes(z)] = summed.astype(BF16)
 
-    z_wait(CONV)
+    from_plane(CONV)
 
     @pl.loop(0, zs)
     def _(z):
-        conv = z_in[CONV, z].astype(F32)
+        conv = picked_turned(z)
         gated_ref[:, lanes(z)] = (shorts[0, z] * conv).astype(BF16)
         pre[0, z, pl.ds(0, tokens)] = cot_ref[:, lanes(z)].astype(F32) * conv
 
+    unloads[0].start()
     edge_copy(0).start()
+    part[...] = jnp.zeros_like(part)
 
     @pl.loop(0, zs)
     def _(z):
-        part[z] = jnp.zeros_like(part[z])
         tap_sums(0, z)
 
     edge_copy(0).wait()
     reverse_conv(0, qgrad_ref)
+    unloads[1].start()
 
     z_wait(DCONV)
 
@@ -342,55 +397,63 @@
     edge_copy(1).start()
     edge_copy(2).start()
 
-    def part_copy(z, slot):
-        return send(part.at[z], part_in.at[slot], part_send.at[z], part_recv.at[slot], at_z(z))
-
-    def plane_copy(g, slot):
-        return send(plane, plane_in.at[slot], plane_send.at[g], plane_recv.at[slot], at_g(g))
-
-    def total_copy(z, slot):
-        return send(plane, total_in.at[slot], total_send.at[z], total_recv.at[slot], at_z(z))
+    share = part.shape[0] // groups
+
+    def shares(g):
+        return pl.ds(g * share, share)
+
+    def part_copy(g, slot):
+        return send(part.at[shares(g)], part_in.at[slot], part_send.at[g], part_recv.at[slot], at_g(g))
+
+    def line_copy(z, slot):
+        return send(plane, line_in.at[slot], line_send.at[z], line_recv.at[slot], at_z(z))
+
+    def total_copy(g, slot):
+        return send(total, total_in.at[shares(slot)], total_send.at[g], total_recv.at[slot], at_g(g))
 
     @pl.loop(0, zs)
     def _(z):
         tap_sums(1, z)
         tap_sums(2, z)
 
+    @pl.loop(1, groups)
+    def _(step):
+        part_copy(g_peer(step), my_g).start()
+
+    part_in[my_g] = part[shares(my_g)]
+
+    @pl.loop(1, groups)
+    def _(step):
+        g = g_peer(groups - step)
+        part_copy(g, g).wait_recv()
+
+    plane[...] = jnp.sum(part_in[...], axis=0)
+
     @pl.loop(1, zs)
     def _(step):
-        part_copy(z_peer(step), my_z).start()
-
-    part_in[my_z] = part[my_z]
+        line_copy(z_peer(step), my_z).start()
+
+    line_in[my_z] = plane[...]
+    send_held_back(DFILTER, late)
     edge_copy(1).wait()
+    reverse_conv(1, kgrad_ref)
+    unloads[2].start()
     edge_copy(2).wait()
-    reverse_conv(1, kgrad_ref)
+    reverse_conv(2, vgrad_ref)
+    unloads[3].start()
 
     @pl.loop(1, zs)
     def _(step):
         z = z_peer(zs - step)
-        part_copy(z, z).wait_recv()
-
-    plane[...] = jnp.sum(part_in[...], axis=0)
+        line_copy(z, z).wait_recv()
+
+    total[...] = jnp.sum(line_in[...], axis=0)
 
     @pl.loop(1, groups)
     def _(step):
-        plane_copy(g_peer(step), my_g).start()
-
-    plane_in[my_g] = plane[...]
-    reverse_conv(2, vgrad_ref)
-
-    @pl.loop(1, groups)
-    def _(step):
-        g = g_peer(groups - step)
-        plane_copy(g, g).wait()
-
-    plane[...] = jnp.sum(plane_in[...], axis=0)
-
-    @pl.loop(1, zs)
-    def _(step):
-        total_copy(z_peer(step), my_z).start()
-
-    total_in[my_z] = plane[...]
+        total_copy(g_peer(step), my_g).start()
+
+    total_in[shares(my_g)] = total[...]
 
     z_wait(DFILTER)
 
@@ -398,15 +461,24 @@
     def _(z):
         fgrad_ref[:, lanes(z)] = z_in[DFILTER, z].astype(F32)
 
-    @pl.loop(1, zs)
-    def _(step):
-        z = z_peer(zs - step)
-        total_copy(z, z).wait()
-        part_copy(z, z).wait_send()
+    unloads[4].start()
+
+    @pl.loop(1, groups)
+    def _(step):
+        g = g_peer(groups - step)
+        total_copy(g, g).wait()
+        part_copy(g, g).wait_send()
 
     for z in range(zs):
         for i in range(3):
-            sgrad_ref[i, :, z * LANES:(z + 1) * LANES] = total_in[z, 3 * i:3 * i + 3]
+            for tap in range(3):
+                sgrad_ref[i, tap:tap + 1, z * LANES:(z + 1) * LANES] = total_in[3 * i + tap, z:z + 1]
+
+    unloads[5].start()
+
+    @pl.loop(1, zs)
+    def _(step):
+        line_copy(z_peer(step), my_z).wait_send()
 
     @pl.loop(0, 6)
     def _(unit):
@@ -417,6 +489,24 @@
         @pl.loop(1, groups)
         def _(step):
             p_copy(unit, g_peer(step)).wait_send()
+
+    for copy in unloads:
+        copy.wait()
+
+
+def store(*refs):
+    *refs, sems = refs
+    count = len(refs) // 3
+    sources, targets, held = refs[:count], refs[count:2 * count], refs[2 * count:]
+    loads = [pltpu.make_async_copy(sources[i], held[i], sems.at[0, i]) for i in range(count)]
+    stores = [pltpu.make_async_copy(held[i], targets[i], sems.at[1, i]) for i in range(count)]
+    for copy in loads:
+        copy.start()
+    for load, copy in zip(loads, stores):
+        load.wait()
+        copy.start()
+    for copy in stores:
+        copy.wait()
 
 
 def shards(factors, query_proj, key_proj, value_proj, cotangent, filter_taps, short_weights):
@@ -426,9 +516,18 @@
     tokens, width = query_proj.shape
     chans = LANES // groups
     scale = 1.0 / math.sqrt(blocks * tokens)
-    whole = pl.BlockSpec(memory_space=pltpu.VMEM)
+    far = pl.BlockSpec(memory_space=pltpu.HBM)
     constants = [jnp.asarray(table) for table in tables(factors)]
-    scratch = [
+    operands = (query_proj, key_proj, value_proj, cotangent, filter_taps, short_weights, *constants)
+    token_out = jax.ShapeDtypeStruct((tokens, width), BF16)
+    outs = (
+        token_out, token_out, token_out, token_out,
+        jax.ShapeDtypeStruct((tokens, width), F32),
+        jax.ShapeDtypeStruct(short_weights.shape, F32),
+    )
+    share = -(-9 // groups)
+    scratch = [pltpu.VMEM(array.shape, array.dtype) for array in (*operands, *outs)]
+    scratch += [
         pltpu.VMEM((3, 16, width), BF16),
         pltpu.VMEM((3, zs, tokens + 8, LANES), F32),
         pltpu.VMEM((3, zs, tokens, LANES), F32),
@@ -442,32 +541,35 @@
         pltpu.VMEM((chans, blocks, 2 * tokens), F32),
         pltpu.VMEM((chans, blocks, 2 * tokens), F32),
         pltpu.VMEM((chans, blocks, 2 * tokens), F32),
-        pltpu.VMEM((zs, 16, LANES), F32),
-        pltpu.VMEM((zs, 16, LANES), F32),
-        pltpu.VMEM((16, LANES), F32),
-        pltpu.VMEM((groups, 16, LANES), F32),
-        pltpu.VMEM((zs, 16, LANES), F32),
+        pltpu.VMEM((groups * share, zs, LANES), F32),
+        pltpu.VMEM((groups, share, zs, LANES), F32),
+        pltpu.VMEM((share, zs, LANES), F32),
+        pltpu.VMEM((zs, share, zs, LANES), F32),
+        pltpu.VMEM((share, zs, LANES), F32),
+        pltpu.VMEM((groups * share, zs, LANES), F32),
     ]
     for shape in (
-        (3,), (3,), (3,), (3,), (6, zs), (6, zs), (6, groups), (6, groups),
-        (zs,), (zs,), (groups,), (groups,), (zs,), (zs,),
+        (len(operands),), (len(outs),), (3,), (3,), (3,), (3,), (6, zs), (6, zs), (6, groups), (6, groups),
+        (groups,), (groups,), (zs,), (zs,), (groups,), (groups,),
     ):
         scratch.append(pltpu.SemaphoreType.DMA(shape))
-    token_out = jax.ShapeDtypeStruct((tokens, width), BF16)
-    return pl.pallas_call(
+    results = pl.pallas_call(
         functools.partial(kernel, factors, scale),
-        out_shape=(
-            token_out, token_out, token_out, token_out,
-            jax.ShapeDtypeStruct((tokens, width), F32),
-            jax.ShapeDtypeStruct(short_weights.shape, F32),
-        ),
-        in_specs=[whole] * 11,
-        out_specs=(whole,) * 6,
+        out_shape=outs,
+        in_specs=[far] * len(operands),
+        out_specs=(far,) * len(outs),
         scratch_shapes=scratch,
         compiler_params=pltpu.CompilerParams(
-            collective_id=0, has_side_effects=True, vmem_limit_bytes=48 * 1024 * 1024
+            collective_id=0, has_side_effects=True, vmem_limit_bytes=VMEM_BYTES
         ),
-    )(query_proj, key_proj, value_proj, cotangent, filter_taps, short_weights, *constants)
+    )(*operands)
+    return pl.pallas_call(
+        store,
+        out_shape=outs,
+        in_specs=[far] * len(outs),
+        out_specs=(far,) * len(outs),
+        scratch_shapes=[pltpu.VMEM(out.shape, out.dtype) for out in outs] + [pltpu.SemaphoreType.DMA((2, len(outs)))],
+    )(*results)
 
 
 def solution(mesh):

time: 132 us -> 108 us (0.82)
  local copies, waits for them, and re-layouts: 14.5 us -> 0 us
  Pallas kernels: 117 us -> 107 us
    unnamed x28 -> x0, local copies, waits for them, and re-layouts: 14.5 us -> none
    pallas_call x1 -> x2, Pallas kernels: 117 us -> 107 us  [the longest x1 105 us: shards(): pl.pallas_call(functools.partial(kernel, factors, scale), out_shape=outs,...]
where the time goes in v2:
time: 108 us
  Pallas kernels  107 us (99%)
    pallas_call x1, Pallas kernels, shards(): pl.pallas_call(functools.partial(kernel, factors, scale), out_shape=outs,...  105 us
    pallas_call x1, Pallas kernels, shards(): pl.pallas_call(store, out_shape=outs, in_specs=[far] * len(outs), out_spe...  2.26 us

profile of v2, /device:TPU:2, one launch (start us, length us, event | category | flops | bytes accessed | tf_op | source)
XLA Modules:
  0.0 107.6 jit_solution(9184962947721809735)
XLA Ops:
  0.6 104.7 %shard_map.154 = (bf16[128,1024]{1,0:T(8,128)(2,1)}, bf16[128,1024]{1,0:T(8,128)(2,1)}, bf16[128,1024]{1,0:T(8,128)(2,1)}, bf16[128,1024]{1,0:T(8,128)(2,1)}, f3...) custom-call(bf16[128,1024]{1,0:T(8,128)(2,1)} %q_hbm.1, bf16[128,1024]{1,0:T(8,128)(2,1)} %k_hbm.1, bf16[128,1024]{1,0:T(8,128)(2,1)} %v_hbm.1, ...), custom_call_target="tpu_custom_call" | custom-call | tf_op jit(solution)/shard_map/pallas_call | solution.py:556
  105.3 2.3 %shard_map.155 = (bf16[128,1024]{1,0:T(8,128)(2,1)}, bf16[128,1024]{1,0:T(8,128)(2,1)}, bf16[128,1024]{1,0:T(8,128)(2,1)}, bf16[128,1024]{1,0:T(8,128)(2,1)}, f3...) custom-call(bf16[128,1024]{1,0:T(8,128)(2,1)} %get-tuple-element.12.refs_0_, bf16[128,1024]{1,0:T(8,128)(2,1)} %get-tuple-element.13.refs_1_, ...), custom_call_target="tpu_custom_call" | custom-call | tf_op jit(solution)/shard_map/pallas_call | solution.py:566

commit v3 on v2

--- a/solution.py
+++ b/solution.py
@@ -335,9 +335,6 @@
     rows_to_plane(DFILTER)
     from_plane(DCONV)
     to_line(DCONV, picked_turned)
-    from_plane(DFILTER)
-    late = 3 * zs // 8
-    to_line(DFILTER, picked_turned, late)
     from_line(CONV, keep)
     to_plane(CONV)
 
@@ -385,6 +382,9 @@
     edge_copy(0).wait()
     reverse_conv(0, qgrad_ref)
     unloads[1].start()
+    from_plane(DFILTER)
+    late = 3 * zs // 8
+    to_line(DFILTER, picked_turned, late)
 
     z_wait(DCONV)
 
@@ -416,24 +416,30 @@
         tap_sums(1, z)
         tap_sums(2, z)
 
-    @pl.loop(1, groups)
-    def _(step):
-        part_copy(g_peer(step), my_g).start()
-
+    active = -(-9 // share)
     part_in[my_g] = part[shares(my_g)]
 
-    @pl.loop(1, groups)
-    def _(step):
-        g = g_peer(groups - step)
-        part_copy(g, g).wait_recv()
-
-    plane[...] = jnp.sum(part_in[...], axis=0)
-
-    @pl.loop(1, zs)
-    def _(step):
-        line_copy(z_peer(step), my_z).start()
-
-    line_in[my_z] = plane[...]
+    @pl.loop(0, active)
+    def _(g):
+        @pl.when(g != my_g)
+        def _():
+            part_copy(g, my_g).start()
+
+    @pl.when(my_g < active)
+    def _():
+        @pl.loop(1, groups)
+        def _(step):
+            g = g_peer(groups - step)
+            part_copy(g, g).wait_recv()
+
+        plane[...] = jnp.sum(part_in[...], axis=0)
+
+        @pl.loop(1, zs)
+        def _(step):
+            line_copy(z_peer(step), my_z).start()
+
+        line_in[my_z] = plane[...]
+
     send_held_back(DFILTER, late)
     edge_copy(1).wait()
     reverse_conv(1, kgrad_ref)
@@ -442,18 +448,20 @@
     reverse_conv(2, vgrad_ref)
     unloads[3].start()
 
-    @pl.loop(1, zs)
-    def _(step):
-        z = z_peer(zs - step)
-        line_copy(z, z).wait_recv()
-
-    total[...] = jnp.sum(line_in[...], axis=0)
-
-    @pl.loop(1, groups)
-    def _(step):
-        total_copy(g_peer(step), my_g).start()
-
-    total_in[shares(my_g)] = total[...]
+    @pl.when(my_g < active)
+    def _():
+        @pl.loop(1, zs)
+        def _(step):
+            z = z_peer(zs - step)
+            line_copy(z, z).wait_recv()
+
+        total[...] = jnp.sum(line_in[...], axis=0)
+
+        @pl.loop(1, groups)
+        def _(step):
+            total_copy(g_peer(step), my_g).start()
+
+        total_in[shares(my_g)] = total[...]
 
     z_wait(DFILTER)
 
@@ -463,11 +471,11 @@
 
     unloads[4].start()
 
-    @pl.loop(1, groups)
-    def _(step):
-        g = g_peer(groups - step)
-        total_copy(g, g).wait()
-        part_copy(g, g).wait_send()
+    @pl.loop(0, active)
+    def _(g):
+        @pl.when(g != my_g)
+        def _():
+            total_copy(g, g).wait_recv()
 
     for z in range(zs):
         for i in range(3):
@@ -476,9 +484,21 @@
 
     unloads[5].start()
 
-    @pl.loop(1, zs)
-    def _(step):
-        line_copy(z_peer(step), my_z).wait_send()
+    @pl.loop(0, active)
+    def _(g):
+        @pl.when(g != my_g)
+        def _():
+            part_copy(g, my_g).wait_send()
+
+    @pl.when(my_g < active)
+    def _():
+        @pl.loop(1, zs)
+        def _(step):
+            line_copy(z_peer(step), my_z).wait_send()
+
+        @pl.loop(1, groups)
+        def _(step):
+            total_copy(g_peer(step), my_g).wait_send()
 
     @pl.loop(0, 6)
     def _(unit):

time: 108 us -> 106 us (0.981)
  the two profiles are of different devices: /device:TPU:2 before, /device:TPU:4 now
where the time goes in v3:
time: 106 us; the launch traced here: 105 us
  Pallas kernels  105 us (99%)
    pallas_call x1, Pallas kernels, shards(): pl.pallas_call(functools.partial(kernel, factors, scale), out_shape=outs,...  103 us
    pallas_call x1, Pallas kernels, shards(): pl.pallas_call(store, out_shape=outs, in_specs=[far] * len(outs), out_spe...  2.26 us

profile of v3, /device:TPU:4, one launch (start us, length us, event | category | flops | bytes accessed | tf_op | source)
XLA Modules:
  0.0 105.5 jit_solution(7494517287313998758)
XLA Ops:
  0.6 102.6 %shard_map.154 = (bf16[128,1024]{1,0:T(8,128)(2,1)}, bf16[128,1024]{1,0:T(8,128)(2,1)}, bf16[128,1024]{1,0:T(8,128)(2,1)}, bf16[128,1024]{1,0:T(8,128)(2,1)}, f3...) custom-call(bf16[128,1024]{1,0:T(8,128)(2,1)} %q_hbm.1, bf16[128,1024]{1,0:T(8,128)(2,1)} %k_hbm.1, bf16[128,1024]{1,0:T(8,128)(2,1)} %v_hbm.1, ...), custom_call_target="tpu_custom_call" | custom-call | tf_op jit(solution)/shard_map/pallas_call | solution.py:576
  103.2 2.3 %shard_map.155 = (bf16[128,1024]{1,0:T(8,128)(2,1)}, bf16[128,1024]{1,0:T(8,128)(2,1)}, bf16[128,1024]{1,0:T(8,128)(2,1)}, bf16[128,1024]{1,0:T(8,128)(2,1)}, f3...) custom-call(bf16[128,1024]{1,0:T(8,128)(2,1)} %get-tuple-element.12.refs_0_, bf16[128,1024]{1,0:T(8,128)(2,1)} %get-tuple-element.13.refs_1_, ...), custom_call_target="tpu_custom_call" | custom-call | tf_op jit(solution)/shard_map/pallas_call | solution.py:586
